TPU v7x, 256 devices: a whole 4x4x8 slice. The times are simulated.
256 devices in a mesh: list: 64 (over z_lo, y, x, core), row: 4 (over z_hi).
Axes of the slice: x: 4, y: 4, z: 8 (z_hi: 4, z_lo: 2; z = z_hi * 2 + z_lo), core: 2. Of those that a mesh axis runs over, the one named last changes fastest.
Arguments:
- corpus: bfloat16 [262144, 768], P(('list', 'row')), may hold values from -6 to 6
- row_list: int32 [262144], P(('list', 'row')), may hold values from 0 to 4095, as said below
- list_slot: int32 [4096], replicated, may hold values from 0 to 4095, as said below
- member_counts: int32 [4096], P('list'), may hold values from 32 to 96, as said below
- old_centroids: float32 [4096, 768], P('list'), may hold values from -6 to 6
- next_rows: bfloat16 [393216, 768], P(('list', 'row')), may hold values from -6 to 6
Outputs:
- new_centroids: float32 [4096, 768], P('list')
- best_score: float32 [393216], P(('list', 'row'))
Inputs may be any that keep to these rules, and one draw needn't show every extreme that they name: `row_list`: each device sends every owner (list_slot // 64) at least 8 and at most 24 of its rows; some owner receives 24 rows from every device. `list_slot`: A permutation of the list numbers. `member_counts`: the exact number of corpus rows in each slot's list; the lists of one owner differ by at most one.
All inputs are finite; a program needn't handle non-finite values.
Results may differ from a plain program's by a relative error of at most 0.0025.
Values may be sent and summed in bfloat16 or wider, within the bound.
A program may use at most 64 MiB of HBM per device.

v0:
```python
import jax
import jax.numpy as jnp
from jax import lax
from jax.sharding import PartitionSpec as P

ITERS = 3
eps_norm = 1e-06
aniso_par = 32.0
perp_weight = 1.0
prior_weight = 16.0


def unit_of(row_block):
    values = row_block.astype(jnp.float32)
    scaled = values / jnp.sqrt(jnp.sum(values * values, axis=1, keepdims=True) + eps_norm)
    return scaled.astype(jnp.bfloat16)


def split_pair(values):
    high_part = values.astype(jnp.bfloat16)
    low_part = (values - high_part.astype(jnp.float32)).astype(jnp.bfloat16)
    return (high_part, low_part)


def prepare(member_block, member_local, lists_own):
    unit_rows = unit_of(member_block)
    membership = (member_local[:, None] == jnp.arange(lists_own, dtype=jnp.int32)[None, :]).astype(
        jnp.float32
    )
    return (unit_rows, membership)


def gram_part(unit_rows, membership, vectors):
    inner_dims = (((1,), (1,)), ((), ()))
    outer_dims = (((0,), (0,)), ((), ()))
    vec_high, vec_low = split_pair(vectors)
    scores = lax.dot_general(unit_rows, vec_high, inner_dims, preferred_element_type=jnp.float32)
    scores = scores + lax.dot_general(
        unit_rows, vec_low, inner_dims, preferred_element_type=jnp.float32
    )
    weighted = scores * membership
    wgt_high, wgt_low = split_pair(weighted)
    result = lax.dot_general(wgt_high, unit_rows, outer_dims, preferred_element_type=jnp.float32)
    return result + lax.dot_general(
        wgt_low, unit_rows, outer_dims, preferred_element_type=jnp.float32
    )


def member_total(membership, member_block):
    return lax.dot_general(
        membership.astype(jnp.bfloat16),
        member_block,
        (((0,), (0,)), ((), ())),
        preferred_element_type=jnp.float32,
    )


def on_device(corpus, row_list, list_slot, member_counts, old_centroids, next_rows):
    n_owner = lax.axis_size("list")
    lists_own = old_centroids.shape[0]
    local_rows = corpus.shape[0]
    cap_slots = 3 * local_rows // (2 * n_owner)
    width = corpus.shape[1]
    slot_ids = jnp.take(list_slot, row_list)
    owner_id = slot_ids // lists_own
    local_id = slot_ids % lists_own
    hits = (owner_id[:, None] == jnp.arange(n_owner, dtype=jnp.int32)[None, :]).astype(jnp.int32)
    rank_in = jnp.sum((jnp.cumsum(hits, axis=0) - 1) * hits, axis=1)
    dest_idx = owner_id * cap_slots + rank_in
    send_rows = (
        jnp.zeros((n_owner * cap_slots, width), jnp.bfloat16)
        .at[dest_idx]
        .set(corpus)
        .reshape(n_owner, cap_slots, width)
    )
    send_local = (
        jnp.full((n_owner * cap_slots,), -1, jnp.int32)
        .at[dest_idx]
        .set(local_id)
        .reshape(n_owner, cap_slots)
    )
    recv_rows, recv_local = (
        lax.all_to_all(send_rows, "list", split_axis=0, concat_axis=0, tiled=True),
        lax.all_to_all(send_local, "list", split_axis=0, concat_axis=0, tiled=True),
    )
    recv_rows = recv_rows.reshape(n_owner * cap_slots, width)
    recv_local = recv_local.reshape(n_owner * cap_slots)
    centroids = old_centroids
    unit_rows, membership = prepare(recv_rows, recv_local, lists_own)
    row_sums, first_gram = lax.psum(
        (member_total(membership, recv_rows), gram_part(unit_rows, membership, centroids)), "row"
    )
    diag_term = perp_weight * member_counts.astype(jnp.float32)[:, None] + prior_weight
    residual = (
        aniso_par * row_sums
        + prior_weight * centroids
        - (diag_term * centroids + (aniso_par - perp_weight) * first_gram)
    )
    direction = residual
    norm_now = jnp.sum(residual * residual, axis=1, keepdims=True)
    for iteration in range(ITERS):
        applied = diag_term * direction + (aniso_par - perp_weight) * lax.psum(
            gram_part(unit_rows, membership, direction), "row"
        )
        step_len = norm_now / jnp.sum(direction * applied, axis=1, keepdims=True)
        centroids = centroids + step_len * direction
        residual = residual - step_len * applied
        norm_next = jnp.sum(residual * residual, axis=1, keepdims=True)
        direction = residual + norm_next / norm_now * direction
        norm_now = norm_next
    panel = centroids.astype(jnp.bfloat16)
    start_score = jnp.full((next_rows.shape[0],), -jnp.inf, jnp.float32)
    piece = lax.all_gather(panel, "list", axis=0, tiled=True)
    piece_rows = piece.shape[0]
    block_size = 512
    blocks = piece.reshape(piece_rows // block_size, block_size, piece.shape[1])

    def one_block(running, piece_block):
        scores = lax.dot_general(
            next_rows, piece_block, (((1,), (1,)), ((), ())), preferred_element_type=jnp.float32
        )
        return (jnp.maximum(running, jnp.max(scores, axis=1)), None)

    result, unused = lax.scan(one_block, start_score, blocks)
    return (centroids, result / width)


def solution(mesh):
    in_specs = (
        P(("list", "row"), None),
        P(("list", "row")),
        P(),
        P("list"),
        P("list", None),
        P(("list", "row"), None),
    )
    out_specs = (P("list", None), P(("list", "row")))
    return jax.shard_map(
        on_device, mesh=mesh, in_specs=in_specs, out_specs=out_specs, check_vma=False
    )
```

profile of v0, /device:TPU:1, one launch (start us, length us, event | category | flops | bytes accessed | tf_op | source)
XLA Modules:
  0.0 470.4 jit_solution(17790374509922220616)
XLA Ops:
  7.2 0.8 fusion.41
  7.9 6.1 %gather_fusion = s32[1024]{0:T(1024)S(1)} fusion(s32[4096]{0:T(1024)S(1)} %copy-done, s32[1024]{0:T(1024)S(1)} %fusion.41), kind=kCustom, calls=%fused_computation | custom fusion | bytes 12288 | tf_op jit(solution)/shard_map/jit(_take)/gather | solution.py:64
  14.2 18.0 %reduce-window.6 = s32[64,8,128]{2,1,0:T(8,128)S(1)} reduce-window(s32[64,8,128]{2,1,0:T(8,128)S(1)} %fusion.11, s32[]{:T(128)} %constant.69.clone.1), window={size=1x1x128 pad=0_0x0_0x127_0}, to_apply=%region_0.1 | reduce-window | flops 8323072 | bytes 524292 | tf_op jit(solution)/shard_map/reduce-window
  32.8 4.3 scatter_custom_fusion
  37.1 0.7 all_to_all.9
  37.8 10.3 %all-to-all-start = ((s32[64,1,24]{2,1,0:T(1,128)}), s32[64,1,24]{2,1,0:T(1,128)S(1)}, u32[]{:S(2)}, u32[]{:S(2)}) async-start(s32[64,1,24]{2,1,0:T(1,128)} %bitcast.3), calls=%async_computation | async-start | bytes 65536 | tf_op jit(solution)/shard_map/all_to_all | solution.py:84
  48.2 7.5 %scatter_custom_fusion.1 = bf16[1536,768]{1,0:T(8,128)(2,1)} fusion(s32[1024]{0:T(1024)S(1)} %compare_select_fusion, bf16[1024,768]{1,0:T(8,128)(2,1)} %param.8, bf16[]{:T(256)} %constant.79.clone.1), kind=kCustom, calls=%fused_computation.18 | custom fusion | bytes 2359808 | tf_op jit(solution)/shard_map/scatter | solution.py:73
  55.9 8.6 %all-to-all-start.1 = ((bf16[64,24,768]{2,1,0:T(8,128)(2,1)}), bf16[64,24,768]{2,1,0:T(8,128)(2,1)S(1)}, u32[]{:S(2)}, u32[]{:S(2)}) async-start(bf16[64,24,768]{2,1,0:T(8,128)(2,1)} %bitcast.46), calls=%async_computation.1 | async-start | bytes 4718592 | tf_op jit(solution)/shard_map/all_to_all | solution.py:83
  65.1 0.7 reduce.5
  65.9 29.0 %all-to-all-done.1 = bf16[64,24,768]{2,1,0:T(8,128)(2,1)S(1)} async-done(((bf16[64,24,768]{2,1,0:T(8,128)(2,1)}), bf16[64,24,768]{2,1,0:T(8,128)(2,1)S(1)}, u32[]{:S(2)}, u32[]{:S(2)}) %all-to-all-start.1) | async-done | bytes 2359328 | tf_op jit(solution)/shard_map/all_to_all | solution.py:83
  95.5 0.9 copy-done.1
  96.5 2.2 divide_convert_fusion
  98.7 0.8 fusion.36
  99.5 0.8 fusion.6
  100.9 1.2 convolution_add_fusion.7
  102.1 1.2 fusion.12
  103.6 52.9 %all-reduce.12.cloned.1.call-done = (f32[64,768]{1,0:T(8,128)}, f32[64,768]{1,0:T(8,128)}) async-done(((f32[64,768]{1,0:T(8,128)}, f32[64,768]{1,0:T(8,128)}), (f32[64,768]{1,0:T(8,128)}, f32[64,768]{1,0:T(8,128)})) %all-reduce.12.cloned.1.call-update) | async-done | bytes 393232 | tf_op jit(solution)/shard_map/psum | solution.py:90
  156.4 1.1 add_subtract_fusion
  157.6 0.8 fusion.33
  158.4 0.8 fusion.5
  159.7 1.2 convolution_add_fusion.6
  161.0 49.5 %all-reduce.6.cloned.1.call-done = f32[64,768]{1,0:T(8,128)} async-done(((f32[64,768]{1,0:T(8,128)}), f32[64,768]{1,0:T(8,128)}) %all-reduce.6.cloned.1.call-update) | async-done | bytes 196624 | tf_op jit(solution)/shard_map/psum | solution.py:102
  210.5 1.1 multiply_reduce_fusion.5
  211.7 1.1 multiply_reduce_fusion.4
  212.9 0.8 fusion.30
  213.8 0.8 fusion.4
  215.1 1.2 convolution_add_fusion.5
  216.4 49.2 %all-reduce.8.cloned.1.call-done = f32[64,768]{1,0:T(8,128)} async-done(((f32[64,768]{1,0:T(8,128)}), f32[64,768]{1,0:T(8,128)}) %all-reduce.8.cloned.1.call-update) | async-done | bytes 196624 | tf_op jit(solution)/shard_map/psum | solution.py:102
  265.6 1.1 multiply_reduce_fusion.3
  266.8 1.1 multiply_reduce_fusion.2
  267.9 1.1 multiply_add_fusion.1
  269.0 0.8 fusion.27
  269.8 0.8 fusion.3
  271.2 1.2 convolution_add_fusion.4
  272.5 49.3 %all-reduce.10.cloned.1.call-done = f32[64,768]{1,0:T(8,128)} async-done(((f32[64,768]{1,0:T(8,128)}), f32[64,768]{1,0:T(8,128)}) %all-reduce.10.cloned.1.call-update) | async-done | bytes 196624 | tf_op jit(solution)/shard_map/psum | solution.py:102
  321.8 1.1 multiply_reduce_fusion.1
  322.9 0.8 fusion.43
  323.7 112.5 %all-gather.2.cloned.1.call-done = bf16[4096,768]{1,0:T(8,128)(2,1)} async-done(((bf16[64,768]{1,0:T(8,128)(2,1)}), bf16[4096,768]{1,0:T(8,128)(2,1)}) %all-gather.2.cloned.1.call-update) | async-done | bytes 6291472 | tf_op jit(solution)/shard_map/all_gather | solution.py:113
  436.2 27.1 %while.11 = (s32[]{:T(128)}, f32[1536]{0:T(1024)S(1)}, bf16[8,512,768]{2,1,0:T(8,128)(2,1)}, bf16[1536,768]{1,0:T(8,128)(2,1)}, s32[]{:T(128)}, /*index=5*/s32[]{:T(128)}) while((s32[]{:T(128)}, f32[1536]{0:T(1024)S(1)}, bf16[8,512,768]{2,1,0:T(8,128)(2,1)}, bf16[1536,768]{1,0:T(8,128)(2,1)}, s32[]{:T(128)}, ...), condition=%wide.region_19.20_spmd.clone, body=%wide.region_17.19_spmd.clone.sunk | while | flops 1208747520 | bytes 3170895 | solution.py:124
  436.2 3.3 convolution_reduce_fusion.2
  439.6 3.3 convolution_reduce_fusion.2
  443.0 3.3 convolution_reduce_fusion.2
  446.4 3.3 convolution_reduce_fusion.2
  449.8 3.3 convolution_reduce_fusion.2
  453.2 3.3 convolution_reduce_fusion.2
  456.5 3.3 convolution_reduce_fusion.2
  459.9 3.3 convolution_reduce_fusion.2
  463.3 0.6 broadcast_multiply_fusion
  (57 shorter events, 4.9 us)
Async XLA Ops:
  7.2 0.8 copy-start
  7.2 6.9 %copy-start.4 = (s32[1024]{0:T(1024)S(1)}, s32[1024]{0:T(1024)}, u32[]{:S(2)}) copy-start(s32[1024]{0:T(1024)} %param.9) | copy-start | bytes 12292
  37.8 18.1 %all-to-all-start = ((s32[64,1,24]{2,1,0:T(1,128)}), s32[64,1,24]{2,1,0:T(1,128)S(1)}, u32[]{:S(2)}, u32[]{:S(2)}) async-start(s32[64,1,24]{2,1,0:T(1,128)} %bitcast.3), calls=%async_computation | async-start | bytes 65536 | tf_op jit(solution)/shard_map/all_to_all | solution.py:84
  55.9 39.0 %all-to-all-start.1 = ((bf16[64,24,768]{2,1,0:T(8,128)(2,1)}), bf16[64,24,768]{2,1,0:T(8,128)(2,1)S(1)}, u32[]{:S(2)}, u32[]{:S(2)}) async-start(bf16[64,24,768]{2,1,0:T(8,128)(2,1)} %bitcast.46), calls=%async_computation.1 | async-start | bytes 4718592 | tf_op jit(solution)/shard_map/all_to_all | solution.py:83
  64.6 91.9 %all-reduce.12.cloned.1.call-start = ((), (), s32[]{:S(2)}) async-start(), calls=%async_computation.6 | async-start | bytes 786432 | tf_op jit(solution)/shard_map/psum | solution.py:90
  95.0 1.4 copy-start.1
  96.5 2.2 copy-start.3
  100.4 1.7 copy-start.2
  100.9 2.7 copy-start.5
  103.3 107.2 %all-reduce.6.cloned.1.call-start = ((), (), s32[]{:S(2)}) async-start(), calls=%async_computation.2 | async-start | bytes 393216 | tf_op jit(solution)/shard_map/psum | solution.py:102
  161.0 104.7 %all-reduce.8.cloned.1.call-start = ((), (), s32[]{:S(2)}) async-start(), calls=%async_computation.3 | async-start | bytes 393216 | tf_op jit(solution)/shard_map/psum | solution.py:102
  216.3 105.4 %all-reduce.10.cloned.1.call-start = ((), (), s32[]{:S(2)}) async-start(), calls=%async_computation.4 | async-start | bytes 393216 | tf_op jit(solution)/shard_map/psum | solution.py:102
  272.4 163.8 %all-gather.2.cloned.1.call-start = ((), (), s32[]{:S(2)}) async-start(), calls=%async_computation.5 | async-start | bytes 6389760 | tf_op jit(solution)/shard_map/all_gather | solution.py:113
Sparse Core Ops, SparseCore 0:
  103.5 52.9 all-reduce.11
  161.1 49.3 all-reduce.5
  216.5 49.1 all-reduce.7
  272.5 49.1 all-reduce.9
  323.9 112.3 all-gather.1
where the time goes:
time: 471 us; the launch traced here: 470 us
  waiting for transfers between devices  343 us (73%)
  matrix products  41.5 us (9%)
  other arithmetic  31.9 us (7%)
  local copies, waits for them, and re-layouts  20.6 us (4%)
  starting transfers between devices  19.3 us (4%)
  between operations  14.1 us (3%)
    psum x3, waiting for transfers between devices, on_device(): lax.psum(gram_part(unit_rows, membership, direction), 'row')  148 us
    all_gather x1, waiting for transfers between devices, on_device(): piece = lax.all_gather(panel, 'list', axis=0, tiled=True)  112 us
    psum x1, waiting for transfers between devices, on_device(): lax.psum((member_total(membership, recv_rows), gram_part(unit_rows, membe...  52.9 us
    all_to_all x1, waiting for transfers between devices, on_device(): lax.all_to_all(send_rows, 'list', split_axis=0, concat_axis=0, tiled=True)  29 us
    dot_general x8, matrix products, one_block(): lax.dot_general(next_rows, piece_block, (((1,), (1,)), ((), ())), preferr...  26.8 us
    another operation x2, other arithmetic  18 us
    all_to_all x1, starting transfers between devices, on_device(): lax.all_to_all(send_local, 'list', split_axis=0, concat_axis=0, tiled=True)  10.3 us
  transfers between devices with their start and end apart: 7, of which 7 were waited for; matrix products, arithmetic and copies ran while one was open for 2% of the time, Pallas kernels for 0%

commit v1 on v0

--- a/solution.py
+++ b/solution.py
@@ -99,8 +99,8 @@
     direction = residual
     norm_now = jnp.sum(residual * residual, axis=1, keepdims=True)
     for iteration in range(ITERS):
-        applied = diag_term * direction + (aniso_par - perp_weight) * lax.psum(
-            gram_part(unit_rows, membership, direction), "row"
+        applied = diag_term * direction + (aniso_par - perp_weight) * jnp.sum(
+            lax.all_gather(gram_part(unit_rows, membership, direction), "row"), axis=0
         )
         step_len = norm_now / jnp.sum(direction * applied, axis=1, keepdims=True)
         centroids = centroids + step_len * direction

time: 471 us -> 378 us (0.80)
  waiting for transfers between devices: 343 us -> 199 us
  blocking collectives: 0 us -> 51.7 us
    psum x3 -> x0, waiting for transfers between devices: 148 us -> none  [on_device(): lax.psum(gram_part(unit_rows, membership, direction), 'row')]
    all_gather x0 -> x3, blocking collectives: none -> 51.7 us  [on_device(): lax.all_gather(gram_part(unit_rows, membership, direction), 'row')]
  transfers between devices with their start and end apart: 7 -> 4, of which waited for: 7 -> 4; matrix products, arithmetic and copies ran while one was open for 2% -> 2% of each run, Pallas kernels for 0% -> 0%
where the time goes in v1:
time: 378 us; the launch traced here: 377 us
  waiting for transfers between devices  199 us (53%)
  blocking collectives  51.7 us (14%)
  matrix products  39.4 us (10%)
  other arithmetic  31.5 us (8%)
  local copies, waits for them, and re-layouts  21.6 us (6%)
  starting transfers between devices  19.2 us (5%)
  between operations  14.5 us (4%)
    all_gather x1, waiting for transfers between devices, on_device(): piece = lax.all_gather(panel, 'list', axis=0, tiled=True)  117 us
    psum x1, waiting for transfers between devices, on_device(): lax.psum((member_total(membership, recv_rows), gram_part(unit_rows, membe...  52.9 us
    all_gather x3, blocking collectives, on_device(): lax.all_gather(gram_part(unit_rows, membership, direction), 'row')  51.7 us
    all_to_all x1, waiting for transfers between devices, on_device(): lax.all_to_all(send_rows, 'list', split_axis=0, concat_axis=0, tiled=True)  29 us
    dot_general x8, matrix products, one_block(): lax.dot_general(next_rows, piece_block, (((1,), (1,)), ((), ())), preferr...  26.8 us
    another operation x2, other arithmetic  18 us
    all_to_all x1, starting transfers between devices, on_device(): lax.all_to_all(send_local, 'list', split_axis=0, concat_axis=0, tiled=True)  10.3 us
    all_to_all x1, starting transfers between devices, on_device(): lax.all_to_all(send_rows, 'list', split_axis=0, concat_axis=0, tiled=True)  8.61 us
  transfers between devices with their start and end apart: 4, of which 4 were waited for; matrix products, arithmetic and copies ran while one was open for 2% of the time, Pallas kernels for 0%

profile of v1, /device:TPU:1, one launch (start us, length us, event | category | flops | bytes accessed | tf_op | source)
XLA Modules:
  0.0 377.1 jit_solution(3369705497837245185)
XLA Ops:
  7.2 0.8 fusion.41
  7.9 6.1 %gather_fusion = s32[1024]{0:T(1024)S(1)} fusion(s32[4096]{0:T(1024)S(1)} %copy-done, s32[1024]{0:T(1024)S(1)} %fusion.41), kind=kCustom, calls=%fused_computation | custom fusion | bytes 12288 | tf_op jit(solution)/shard_map/jit(_take)/gather | solution.py:64
  14.2 18.0 %reduce-window.6 = s32[64,8,128]{2,1,0:T(8,128)S(1)} reduce-window(s32[64,8,128]{2,1,0:T(8,128)S(1)} %fusion.11, s32[]{:T(128)} %constant.69.clone.1), window={size=1x1x128 pad=0_0x0_0x127_0}, to_apply=%region_0.1 | reduce-window | flops 8323072 | bytes 524292 | tf_op jit(solution)/shard_map/reduce-window
  32.8 4.3 %scatter_custom_fusion = s32[1536]{0:T(1024)S(1)} fusion(s32[1024]{0:T(1024)S(1)} %compare_select_fusion, s32[1024]{0:T(1024)S(1)} %get-tuple-element.56, s32[]{:T(128)} %constant.68.clone.1), kind=kCustom, calls=%fused_computation.91 | custom fusion | bytes 6148 | tf_op jit(solution)/shard_map/scatter | solution.py:79
  37.1 0.7 all_to_all.9
  37.8 10.3 %all-to-all-start = ((s32[64,1,24]{2,1,0:T(1,128)}), s32[64,1,24]{2,1,0:T(1,128)S(1)}, u32[]{:S(2)}, u32[]{:S(2)}) async-start(s32[64,1,24]{2,1,0:T(1,128)} %bitcast.3), calls=%async_computation | async-start | bytes 65536 | tf_op jit(solution)/shard_map/all_to_all | solution.py:84
  48.2 7.5 %scatter_custom_fusion.1 = bf16[1536,768]{1,0:T(8,128)(2,1)} fusion(s32[1024]{0:T(1024)S(1)} %compare_select_fusion, bf16[1024,768]{1,0:T(8,128)(2,1)} %param.8, bf16[]{:T(256)} %constant.79.clone.1), kind=kCustom, calls=%fused_computation.18 | custom fusion | bytes 2359808 | tf_op jit(solution)/shard_map/scatter | solution.py:73
  55.9 8.6 %all-to-all-start.1 = ((bf16[64,24,768]{2,1,0:T(8,128)(2,1)}), bf16[64,24,768]{2,1,0:T(8,128)(2,1)S(1)}, u32[]{:S(2)}, u32[]{:S(2)}) async-start(bf16[64,24,768]{2,1,0:T(8,128)(2,1)} %bitcast.49), calls=%async_computation.1 | async-start | bytes 4718592 | tf_op jit(solution)/shard_map/all_to_all | solution.py:83
  65.1 0.7 reduce.5
  66.0 29.0 %all-to-all-done.1 = bf16[64,24,768]{2,1,0:T(8,128)(2,1)S(1)} async-done(((bf16[64,24,768]{2,1,0:T(8,128)(2,1)}), bf16[64,24,768]{2,1,0:T(8,128)(2,1)S(1)}, u32[]{:S(2)}, u32[]{:S(2)}) %all-to-all-start.1) | async-done | bytes 2359328 | tf_op jit(solution)/shard_map/all_to_all | solution.py:83
  95.0 0.5 multiply_reduce_fusion
  95.5 0.9 copy-done.1
  96.5 2.2 divide_convert_fusion
  98.7 0.8 fusion.36
  99.5 0.8 fusion.6
  100.9 1.2 convolution_add_fusion.7
  102.1 1.2 fusion.12
  103.6 52.9 %all-reduce.3.cloned.1.call-done = (f32[64,768]{1,0:T(8,128)}, f32[64,768]{1,0:T(8,128)}) async-done(((f32[64,768]{1,0:T(8,128)}, f32[64,768]{1,0:T(8,128)}), (f32[64,768]{1,0:T(8,128)}, f32[64,768]{1,0:T(8,128)})) %all-reduce.3.cloned.1.call-update) | async-done | bytes 393232 | tf_op jit(solution)/shard_map/psum | solution.py:90
  156.4 1.1 add_subtract_fusion
  157.6 0.8 fusion.33
  158.4 0.8 fusion.5
  159.7 0.5 convolution_add_fusion.6
  160.3 16.9 %all-gather = f32[256,768]{1,0:T(8,128)S(1)} all-gather(f32[64,768]{1,0:T(8,128)S(1)} %convolution_add_fusion.6), channel_id=2, replica_groups=mesh['list'=64,'row'=4] {'row'}, dimensions={0}, use_global_device_ids=true | all-gather | bytes 983040 | tf_op jit(solution)/shard_map/all_gather | solution.py:103
  177.2 0.7 reduce_sum.102
  177.9 1.1 multiply_reduce_fusion.5
  179.1 1.1 multiply_reduce_fusion.4
  180.8 0.8 fusion.30
  181.7 0.8 fusion.4
  183.0 0.5 convolution_add_fusion.5
  183.6 18.2 %all-gather.1 = f32[256,768]{1,0:T(8,128)} all-gather(f32[64,768]{1,0:T(8,128)S(1)} %convolution_add_fusion.5), channel_id=3, replica_groups=mesh['list'=64,'row'=4] {'row'}, dimensions={0}, use_global_device_ids=true | all-gather | bytes 983040 | tf_op jit(solution)/shard_map/all_gather | solution.py:103
  201.8 1.2 reduce_sum.105
  203.0 0.9 multiply_reduce_fusion.3
  204.6 0.8 multiply_add_fusion.1
  205.4 0.8 fusion.27
  206.3 0.8 fusion.3
  208.2 16.6 %all-gather.2 = f32[256,768]{1,0:T(8,128)S(1)} all-gather(f32[64,768]{1,0:T(8,128)S(1)} %convolution_add_fusion.4), channel_id=4, replica_groups=mesh['list'=64,'row'=4] {'row'}, dimensions={0}, use_global_device_ids=true | all-gather | bytes 983040 | tf_op jit(solution)/shard_map/all_gather | solution.py:103
  225.0 0.8 fusion.43
  225.9 116.8 %all-gather.5.cloned.1.call-done = bf16[4096,768]{1,0:T(8,128)(2,1)} async-done(((bf16[64,768]{1,0:T(8,128)(2,1)}), bf16[4096,768]{1,0:T(8,128)(2,1)}) %all-gather.5.cloned.1.call-update) | async-done | bytes 6291472 | tf_op jit(solution)/shard_map/all_gather | solution.py:113
  342.6 27.1 %while.11 = (s32[]{:T(128)}, f32[1536]{0:T(1024)S(1)}, bf16[8,512,768]{2,1,0:T(8,128)(2,1)}, bf16[1536,768]{1,0:T(8,128)(2,1)}, s32[]{:T(128)}, /*index=5*/s32[]{:T(128)}) while((s32[]{:T(128)}, f32[1536]{0:T(1024)S(1)}, bf16[8,512,768]{2,1,0:T(8,128)(2,1)}, bf16[1536,768]{1,0:T(8,128)(2,1)}, s32[]{:T(128)}, ...), condition=%wide.region_19.20_spmd.clone, body=%wide.region_17.19_spmd.clone.sunk | while | flops 1208747520 | bytes 3170895 | solution.py:124
  342.6 3.3 convolution_reduce_fusion.2
  346.0 3.3 convolution_reduce_fusion.2
  349.4 3.3 convolution_reduce_fusion.2
  352.8 3.3 convolution_reduce_fusion.2
  356.1 3.3 convolution_reduce_fusion.2
  359.5 3.3 convolution_reduce_fusion.2
  362.9 3.3 convolution_reduce_fusion.2
  366.3 3.3 convolution_reduce_fusion.2
  369.7 0.6 broadcast_multiply_fusion
  (82 shorter events, 6.2 us)
Async XLA Ops:
  7.2 0.8 copy-start
  7.2 6.9 %copy-start.10 = (s32[1024]{0:T(1024)S(1)}, s32[1024]{0:T(1024)}, u32[]{:S(2)}) copy-start(s32[1024]{0:T(1024)} %param.9) | copy-start | bytes 12292
  37.8 18.1 %all-to-all-start = ((s32[64,1,24]{2,1,0:T(1,128)}), s32[64,1,24]{2,1,0:T(1,128)S(1)}, u32[]{:S(2)}, u32[]{:S(2)}) async-start(s32[64,1,24]{2,1,0:T(1,128)} %bitcast.3), calls=%async_computation | async-start | bytes 65536 | tf_op jit(solution)/shard_map/all_to_all | solution.py:84
  55.9 39.0 %all-to-all-start.1 = ((bf16[64,24,768]{2,1,0:T(8,128)(2,1)}), bf16[64,24,768]{2,1,0:T(8,128)(2,1)S(1)}, u32[]{:S(2)}, u32[]{:S(2)}) async-start(bf16[64,24,768]{2,1,0:T(8,128)(2,1)} %bitcast.49), calls=%async_computation.1 | async-start | bytes 4718592 | tf_op jit(solution)/shard_map/all_to_all | solution.py:83
  64.6 91.9 %all-reduce.3.cloned.1.call-start = ((), (), s32[]{:S(2)}) async-start(), calls=%async_computation.3 | async-start | bytes 786432 | tf_op jit(solution)/shard_map/psum | solution.py:90
  65.9 92.4 %copy-start.4 = (s32[1536]{0:T(1024)}, s32[1536]{0:T(1024)S(1)}, u32[]{:S(2)}) copy-start(s32[1536]{0:T(1024)S(1)} %eq.47) | copy-start | bytes 18436
  95.0 1.4 copy-start.1
  96.5 2.2 copy-start.3
  100.4 1.7 copy-start.2
  100.9 2.7 copy-start.19
  103.3 239.3 %all-gather.5.cloned.1.call-start = ((), (), s32[]{:S(2)}) async-start(), calls=%async_computation.2 | async-start | bytes 6389760 | tf_op jit(solution)/shard_map/all_gather | solution.py:113
  103.6 55.6 %copy-start.7 = (f32[64]{0:T(128)}, f32[64]{0:T(128)S(1)}, u32[]{:S(2)}) copy-start(f32[64]{0:T(128)S(1)} %convert_add_fusion) | copy-start | bytes 772
  177.9 3.8 copy-start.5
  179.1 1.2 copy-start.13
  180.2 0.5 copy-start.17
  183.6 20.3 %copy-start.18 = (f32[64]{0:T(128)S(1)}, f32[64]{0:T(128)}, u32[]{:S(2)}) copy-start(f32[64]{0:T(128)} %copy-done.17) | copy-start | bytes 772
  183.6 20.3 %copy-start.8 = (f32[64]{0:T(128)S(1)}, f32[64]{0:T(128)}, u32[]{:S(2)}) copy-start(f32[64]{0:T(128)} %copy-done.7) | copy-start | bytes 772
  203.0 3.3 copy-start.6
  203.9 0.7 copy-start.11
  204.1 0.5 copy-start.15
  207.6 17.2 %copy-start.9 = (f32[64]{0:T(128)S(1)}, f32[64]{0:T(128)}, u32[]{:S(2)}) copy-start(f32[64]{0:T(128)} %copy-done.7) | copy-start | bytes 772
  207.6 17.4 %copy-start.16 = (f32[64]{0:T(128)S(1)}, f32[64]{0:T(128)}, u32[]{:S(2)}) copy-start(f32[64]{0:T(128)} %copy-done.15) | copy-start | bytes 772
  207.6 17.4 %copy-start.12 = (f32[64]{0:T(128)S(1)}, f32[64]{0:T(128)}, u32[]{:S(2)}) copy-start(f32[64]{0:T(128)} %copy-done.11) | copy-start | bytes 772
  207.6 17.4 %copy-start.14 = (f32[64]{0:T(128)S(1)}, f32[64]{0:T(128)}, u32[]{:S(2)}) copy-start(f32[64]{0:T(128)} %copy-done.13) | copy-start | bytes 772
Sparse Core Ops, SparseCore 0:
  103.5 52.9 all-reduce.2
  226.0 116.5 all-gather.4
